TPU v7x, 512 devices: a whole 4x8x8 slice. The times are simulated.
512 devices in a mesh: seq: 32 (over x, y_lo, core), res: 16 (over y_hi, z).
Axes of the slice: x: 4, y: 8 (y_hi: 2, y_lo: 4; y = y_hi * 4 + y_lo), z: 8, core: 2. Of those that a mesh axis runs over, the one named last changes fastest.
Arguments:
- alignment: bfloat16 [256, 512, 768], P('seq', 'res'), may hold values from -6 to 6
- row_gain: bfloat16 [768], replicated, may hold values from 0.099609375 to 1.8984375
- row_project: bfloat16 [768, 1152], replicated, may hold values from -4 to 4
- row_output: bfloat16 [384, 768], replicated, may hold values from -2.5 to 2.5
- column_gain: bfloat16 [768], replicated, may hold values from 0.099609375 to 1.8984375
- column_project: bfloat16 [768, 1152], replicated, may hold values from -4 to 4
Outputs:
- row_updated: bfloat16 [256, 512, 768], P('seq', 'res')
- column_context: bfloat16 [256, 512, 384], P('seq', 'res')
All inputs are finite; a program needn't handle non-finite values.
Results may differ from a plain program's by a relative error of at most 0.025.
Values may be sent and summed in bfloat16 or wider, within the bound.
A program may use at most 64 MiB of HBM per device.

v0:
```python
import math

import jax
import jax.numpy as jnp
from jax import lax
from jax.sharding import PartitionSpec as P

HEADS = 6
HEAD = 64


def layer_norm(values, gain):
    average = jnp.mean(values, axis=-1, keepdims=True)
    centred = values - average
    spread = jnp.mean(centred * centred, axis=-1, keepdims=True)
    return centred * lax.rsqrt(spread + 1e-05) * gain.astype(jnp.float32)


def body(alignment, row_gain, row_project, row_output, column_gain, column_project):
    rows_here, cols_here, features = alignment.shape
    inner = HEADS * HEAD
    source = alignment.astype(jnp.float32)
    normed = layer_norm(source, row_gain).astype(jnp.bfloat16)
    packed = jnp.dot(
        normed.reshape(rows_here * cols_here, features),
        row_project,
        preferred_element_type=jnp.float32,
    ).astype(jnp.bfloat16)
    packed = packed.reshape(rows_here, cols_here, 3 * inner)
    queries = packed[:, :, :inner].reshape(rows_here, cols_here, HEADS, HEAD)
    keys_local = packed[:, :, inner : 2 * inner]
    values_local = packed[:, :, 2 * inner :]
    seq_count = lax.axis_size("seq")
    scaling = 1.0 / (math.sqrt(HEAD) * math.sqrt(rows_here * seq_count))
    panel = lax.all_gather(keys_local, "res", axis=1, tiled=True)
    panel_cols = panel.shape[1]
    partial_value = jnp.einsum(
        "rihe,rjhe->hij",
        queries,
        panel.reshape(rows_here, panel_cols, HEADS, HEAD),
        preferred_element_type=jnp.float32,
    )
    summed = lax.psum(partial_value, "seq")
    tied = jax.nn.softmax(summed * scaling, axis=-1).astype(jnp.bfloat16)
    panel = lax.all_gather(values_local, "res", axis=1, tiled=True)
    panel_cols = panel.shape[1]
    context = jnp.einsum(
        "hij,rjhe->rihe",
        tied,
        panel.reshape(rows_here, panel_cols, HEADS, HEAD),
        preferred_element_type=jnp.float32,
    )
    context = context.astype(jnp.bfloat16)
    update = jnp.dot(
        context.reshape(rows_here * cols_here, inner),
        row_output,
        preferred_element_type=jnp.float32,
    )
    row_updated = (source + update.reshape(rows_here, cols_here, features)).astype(jnp.bfloat16)
    normed_col = layer_norm(row_updated.astype(jnp.float32), column_gain).astype(jnp.bfloat16)
    packed_col = jnp.dot(
        normed_col.reshape(rows_here * cols_here, features),
        column_project,
        preferred_element_type=jnp.float32,
    ).astype(jnp.bfloat16)
    per_device = cols_here // seq_count
    packed_col = packed_col.reshape(rows_here, seq_count, per_device, 3 * inner)
    block = lax.all_to_all(packed_col, "seq", split_axis=1, concat_axis=0, tiled=True)
    rows_all = block.shape[0]
    items = block.shape[2]
    parts = block.reshape(rows_all, items, 3, HEADS, HEAD)
    scores = jnp.einsum(
        "rche,sche->chrs", parts[:, :, 0], parts[:, :, 1], preferred_element_type=jnp.float32
    ) * (1.0 / math.sqrt(HEAD))
    weights = jax.nn.softmax(scores, axis=-1).astype(jnp.bfloat16)
    attended = jnp.einsum(
        "chrs,sche->rche", weights, parts[:, :, 2], preferred_element_type=jnp.float32
    ).astype(jnp.bfloat16)
    attended = attended.reshape(rows_all, 1, items, inner)
    gathered = lax.all_to_all(attended, "seq", split_axis=0, concat_axis=1, tiled=True)
    column_context = gathered.reshape(rows_here, cols_here, inner)
    return (row_updated, column_context)


def solution(mesh):
    placed = (P("seq", "res", None), P(), P(), P(), P(), P())
    return jax.shard_map(
        body,
        mesh=mesh,
        in_specs=placed,
        out_specs=(P("seq", "res", None), P("seq", "res", None)),
        check_vma=False,
    )
```

profile of v0, /device:TPU:1, one launch (start us, length us, event | category | flops | bytes accessed | tf_op | source)
XLA Modules:
  0.0 589.4 jit_solution(6682550106655648141)
XLA Ops:
  7.2 1.2 convert_reduce_fusion
  8.5 1.2 fusion.24
  9.7 0.7 convert_element_type.50
  10.4 1.2 fusion.26
  11.7 0.7 convolution_convert_fusion.1
  12.4 0.7 copy.43
  13.2 0.7 copy.42
  14.0 0.3 reshape.103
  14.3 118.4 %all-gather.5.cloned.1.call-done = bf16[8,512,384]{2,0,1:T(8,128)(2,1)} async-done(((bf16[8,32,384]{2,0,1:T(8,128)(2,1)}), bf16[8,512,384]{2,0,1:T(8,128)(2,1)}) %all-gather.5.cloned.1.call-update) | async-done | bytes 3145744 | tf_op jit(solution)/shard_map/all_gather | solution.py:35
  132.8 5.1 copy.26
  137.9 3.3 fusion.14
  141.2 108.8 %all-gather.3.cloned.1.call-done = bf16[8,512,384]{2,0,1:T(8,128)(2,1)} async-done(((bf16[8,32,384]{2,0,1:T(8,128)(2,1)}), bf16[8,512,384]{2,0,1:T(8,128)(2,1)}) %all-gather.3.cloned.1.call-update) | async-done | bytes 3145744 | tf_op jit(solution)/shard_map/all_gather | solution.py:45
  250.0 5.0 copy.24
  255.0 267.3 %all-reduce.2.cloned.1.call-done = f32[6,32,512]{2,1,0:T(8,128)} async-done(((f32[6,32,512]{2,1,0:T(8,128)}), f32[6,32,512]{2,1,0:T(8,128)}) %all-reduce.2.cloned.1.call-update) | async-done | bytes 393232 | tf_op jit(solution)/shard_map/psum | solution.py:43
  522.3 1.2 fusion.58
  523.5 4.3 fusion.17
  527.8 1.4 copy.30
  529.2 0.3 dot_general.26
  529.5 0.4 convert_reduce_fusion.1
  530.3 0.5 copy-done.2
  531.1 0.7 convolution_convert_fusion
  532.0 25.5 %all_to_all.30 = bf16[8,32,1,1152]{3,0,2,1:T(8,128)(2,1)} all-to-all(bf16[8,32,1,1152]{3,0,2,1:T(8,128)(2,1)S(1)} %copy.31), channel_id=1, replica_groups=mesh['seq'=32,'res'=16] {'seq'}, dimensions={1} | all-to-all | bytes 1179648 | tf_op jit(solution)/shard_map/all_to_all | solution.py:68
  557.5 1.9 reshape.107
  559.4 1.3 fusion.56
  560.6 1.3 copy.45
  562.0 1.3 copy.46
  563.6 1.8 fusion.59
  565.4 1.7 convolution_convert_fusion.2
  567.0 0.5 broadcast.59
  567.5 0.8 reduce.4
  568.6 13.4 %all_to_all.31 = bf16[32,2,1536]{2,1,0:T(2,128)(2,1)S(1)} all-to-all(bf16[32,2,1536]{2,1,0:T(2,128)(2,1)S(1)} %reshape.116), channel_id=1, replica_groups=mesh['seq'=32,'res'=16] {'seq'}, dimensions={0} | all-to-all | bytes 393216 | tf_op jit(solution)/shard_map/all_to_all | solution.py:80
  582.2 0.7 copy.37
  (33 shorter events, 1.8 us)
Async XLA Ops:
  7.2 4.5 copy-start
  7.2 125.6 %all-gather.5.cloned.1.call-start = ((), (), s32[]{:S(2)}) async-start(), calls=%async_computation.3 | async-start | bytes 3342336 | tf_op jit(solution)/shard_map/all_gather | solution.py:35
  13.2 236.8 %all-gather.3.cloned.1.call-start = ((), (), s32[]{:S(2)}) async-start(), calls=%async_computation.2 | async-start | bytes 3342336 | tf_op jit(solution)/shard_map/all_gather | solution.py:45
  14.0 508.3 %all-reduce.2.cloned.1.call-start = ((), (), s32[]{:S(2)}) async-start(), calls=%async_computation.4 | async-start | bytes 786432 | tf_op jit(solution)/shard_map/psum | solution.py:43
  137.9 3.3 copy-start.5
  527.8 1.7 copy-start.1
  527.8 1.7 copy-start.4
  529.5 1.6 copy-start.6
  530.0 0.8 copy-start.2
  560.6 2.6 copy-start.3
Sparse Core Ops, SparseCore 0:
  13.3 119.4 all-gather.4
  136.5 113.4 all-gather.2
  253.5 268.7 all-reduce.1
where the time goes:
time: 590 us; the launch traced here: 589 us
  waiting for transfers between devices  495 us (84%)
  blocking collectives  38.9 us (7%)
  local copies, waits for them, and re-layouts  22.2 us (4%)
  between operations  14 us (2%)
  matrix products  12.9 us (2%)
  other arithmetic  6.81 us (1%)
    psum x1, waiting for transfers between devices, body(): summed = lax.psum(partial_value, 'seq')  267 us
    all_gather x1, waiting for transfers between devices, body(): panel = lax.all_gather(keys_local, 'res', axis=1, tiled=True)  118 us
    all_gather x1, waiting for transfers between devices, body(): panel = lax.all_gather(values_local, 'res', axis=1, tiled=True)  109 us
    all_to_all x1, blocking collectives, body(): lax.all_to_all(packed_col, 'seq', split_axis=1, concat_axis=0, tiled=True)  25.5 us
    all_to_all x1, blocking collectives, body(): lax.all_to_all(attended, 'seq', split_axis=0, concat_axis=1, tiled=True)  13.4 us
  transfers between devices with their start and end apart: 3, of which 3 were waited for; matrix products, arithmetic and copies ran while one was open for 2% of the time, Pallas kernels for 0%

commit v1 on v0

v1 whole, which is shorter than its diff:
```python
import functools
import math

import jax
import jax.numpy as jnp
from jax import lax
from jax.experimental import pallas as pl
from jax.experimental.pallas import tpu as pltpu
from jax.sharding import PartitionSpec as P

HEADS = 6
HEAD = 64
INNER = HEADS * HEAD
LANES = 128
Z = 8
MESH = pl.DeviceIdType.MESH


def layer_norm(values, gain):
    average = jnp.mean(values, axis=-1, keepdims=True)
    centred = values - average
    spread = jnp.mean(centred * centred, axis=-1, keepdims=True)
    return centred * lax.rsqrt(spread + 1e-05) * gain.astype(jnp.float32)


def low_lanes(shape):
    return lax.broadcasted_iota(jnp.int32, shape, len(shape) - 1) < HEAD


def arrived(ref, sem):
    pltpu.make_async_copy(ref, ref, sem).wait()


def kernel(
    seqs, x_ref, g1_ref, w1_ref, g2_ref, wo_hbm, w2_hbm, ru_ref, cc_ref,
    wo_ref, w2_ref, tiles, rq, rk, rv, lp, rl, td, rt, oc, rc, pc, rp, ac, ra,
    load_sem, out_q, out_k, out_v, in_qkv, out_c, in_c, out_seq, in_seq,
):
    rows, cols, features = x_ref.shape
    tokens = rows * cols
    half = tokens // 2
    res = 2 * Z
    here = Z * cols
    everywhere = res * cols
    share = here // seqs
    per_device = cols // seqs
    f32, bf16 = jnp.float32, jnp.bfloat16

    s = lax.axis_index("seq")
    t = lax.axis_index("res")
    yh = t // Z
    z = t % Z
    worker = z % 4 != 3
    head_here = z - z // 4

    barrier = pltpu.get_barrier_semaphore()

    def greet_seq(k, carry):
        pl.semaphore_signal(barrier, inc=1, device_id={"seq": lax.rem(s + k, seqs)}, device_id_type=MESH)
        return carry

    def greet_res(k, carry):
        pl.semaphore_signal(barrier, inc=1, device_id={"res": lax.rem(t + k, res)}, device_id_type=MESH)
        return carry

    lax.fori_loop(1, seqs, greet_seq, 0)
    lax.fori_loop(1, res, greet_res, 0)

    load_wo = pltpu.make_async_copy(wo_hbm, wo_ref, load_sem.at[0])
    load_w2 = pltpu.make_async_copy(w2_hbm, w2_ref, load_sem.at[1])
    load_wo.start()
    load_w2.start()

    source = x_ref[...].reshape(tokens, features).astype(f32)
    normed = layer_norm(source, g1_ref[...]).astype(bf16)

    def project(part):
        packed = jnp.dot(normed, w1_ref[:, part * INNER : (part + 1) * INNER], preferred_element_type=f32)
        for pair in range(HEADS // 2):
            tile = packed[:, pair * LANES : (pair + 1) * LANES]
            turned = pltpu.roll(tile, HEAD, 1)
            low = low_lanes((half, LANES))
            first = jnp.where(low, tile[:half], turned[half:]).astype(bf16)
            second = jnp.where(low, turned[:half], tile[half:]).astype(bf16)
            tiles[part, 2 * pair] = first.reshape(rows // 2, cols, LANES)
            tiles[part, 2 * pair + 1] = second.reshape(rows // 2, cols, LANES)

    def send_head(part, dst, slot, send, recv, both):
        def step(h, carry):
            at = h + h // 3
            block = tiles.at[part, h]

            @pl.when(z == at)
            def _():
                pltpu.make_async_copy(block, dst.at[slot], recv).start()

            @pl.when(z != at)
            def _():
                pltpu.make_async_remote_copy(
                    block, dst.at[slot], send.at[h, 0], recv,
                    device_id={"res": yh * Z + at}, device_id_type=MESH,
                ).start()

            if both:
                pltpu.make_async_remote_copy(
                    block, dst.at[slot], send.at[h, 1], recv,
                    device_id={"res": (1 - yh) * Z + at}, device_id_type=MESH,
                ).start()
            return carry

        lax.fori_loop(0, HEADS, step, 0)

    def sent_head(part, send, both):
        def step(h, carry):
            at = h + h // 3
            block = tiles.at[part, h]

            @pl.when(z != at)
            def _():
                arrived(block, send.at[h, 0])

            if both:
                arrived(block, send.at[h, 1])
            return carry

        lax.fori_loop(0, HEADS, step, 0)

    def exchange(block, dst, stage):
        pltpu.make_async_copy(block(s), dst.at[s], in_seq.at[stage]).start()

        def step(k, carry):
            peer = lax.rem(s + k, seqs)
            pltpu.make_async_remote_copy(
                block(peer), dst.at[s], out_seq.at[stage], in_seq.at[stage],
                device_id={"seq": peer}, device_id_type=MESH,
            ).start()
            return carry

        lax.fori_loop(1, seqs, step, 0)

    def sent(dst, stage):
        arrived(dst.at[pl.ds(0, seqs - 1)], out_seq.at[stage])

    project(1)
    pl.semaphore_wait(barrier, seqs + res - 2)
    send_head(1, rk, t, out_k, in_qkv.at[1], True)
    project(0)
    send_head(0, rq, z, out_q, in_qkv.at[0], False)
    project(2)
    send_head(2, rv, t, out_v, in_qkv.at[2], True)

    @pl.when(worker)
    def _():
        arrived(rk, in_qkv.at[1])
        arrived(rq, in_qkv.at[0])
        quads = rows // 2
        queries = jnp.concatenate([rq[:, r].reshape(here, LANES) for r in range(quads)], axis=1)
        keys = jnp.concatenate([rk[:, r].reshape(everywhere, LANES) for r in range(quads)], axis=1)
        logits = lax.dot_general(
            queries, keys, (((1,), (1,)), ((), ())), preferred_element_type=f32
        ) * (1.0 / (math.sqrt(HEAD) * math.sqrt(rows * seqs)))
        logits = logits.reshape(seqs, share, everywhere)
        lp[...] = jnp.concatenate([logits[:, :, :here], logits[:, :, here:]], axis=1).astype(bf16)
        exchange(lambda peer: lp.at[peer], rl, 0)
        arrived(rl, in_seq.at[0])
        total = jnp.sum(rl[...].astype(f32), axis=0)
        left, right = total[:share], total[share:]
        most = jnp.maximum(
            jnp.max(left, axis=-1, keepdims=True), jnp.max(right, axis=-1, keepdims=True)
        )
        left, right = jnp.exp(left - most), jnp.exp(right - most)
        norm = jnp.sum(left, axis=-1, keepdims=True) + jnp.sum(right, axis=-1, keepdims=True)
        td[...] = jnp.concatenate([left / norm, right / norm], axis=0).astype(bf16)
        exchange(lambda peer: td, rt, 1)
        arrived(rv, in_qkv.at[2])
        values = jnp.concatenate([rv[:, r].reshape(everywhere, LANES) for r in range(quads)], axis=1)
        arrived(rt, in_seq.at[1])
        tied = rt[...].astype(f32)
        left = tied[:, :share].reshape(here, here).astype(bf16)
        right = tied[:, share:].reshape(here, here).astype(bf16)
        context = jnp.dot(left, values[:here], preferred_element_type=f32)
        context += jnp.dot(right, values[here:], preferred_element_type=f32)
        for r in range(quads):
            oc[:, r] = context[:, r * LANES : (r + 1) * LANES].reshape(Z, cols, LANES).astype(bf16)
        pltpu.make_async_copy(oc.at[z], rc.at[head_here], in_c).start()

        def step(k, carry):
            peer = lax.rem(z + k, Z)
            pltpu.make_async_remote_copy(
                oc.at[peer], rc.at[head_here], out_c, in_c,
                device_id={"res": yh * Z + peer}, device_id_type=MESH,
            ).start()
            return carry

        lax.fori_loop(1, Z, step, 0)

    load_wo.wait()
    load_w2.wait()
    arrived(rc, in_c)
    low = low_lanes((half, LANES))
    tops, bottoms = [], []
    for pair in range(HEADS // 2):
        first = rc[2 * pair].reshape(half, LANES).astype(f32)
        second = rc[2 * pair + 1].reshape(half, LANES).astype(f32)
        tops.append(jnp.where(low, first, pltpu.roll(second, HEAD, 1)).astype(bf16))
        bottoms.append(jnp.where(low, pltpu.roll(first, HEAD, 1), second).astype(bf16))
    context = jnp.concatenate(
        [jnp.concatenate(tops, axis=1), jnp.concatenate(bottoms, axis=1)], axis=0
    )
    update = jnp.dot(context, wo_ref[...], preferred_element_type=f32)
    source = x_ref[...].reshape(tokens, features).astype(f32)
    row_updated = (source + update).astype(bf16)
    ru_ref[...] = row_updated.reshape(rows, cols, features)
    normed = layer_norm(row_updated.astype(f32), g2_ref[...]).astype(bf16)
    one = lax.broadcasted_iota(jnp.int32, (tokens, tokens), 0)
    two = lax.broadcasted_iota(jnp.int32, (tokens, tokens), 1)
    turn = jnp.where((one % rows) * cols + one // rows == two, 1.0, 0.0).astype(bf16)
    normed = jnp.dot(turn, normed, preferred_element_type=f32).astype(bf16)
    for part in range(3):
        span = slice(part * INNER, (part + 1) * INNER)
        packed = jnp.dot(normed, w2_ref[:, span], preferred_element_type=f32).astype(bf16)
        pc[:, :, :, span] = packed.reshape(seqs, per_device, rows, INNER)
    exchange(lambda peer: pc.at[peer], rp, 2)
    arrived(rp, in_seq.at[2])
    total_rows = seqs * rows
    low = low_lanes((total_rows, LANES))
    zero = jnp.zeros((total_rows, LANES), bf16)
    for c in range(per_device):
        for pair in range(HEADS // 2):
            span = slice(pair * LANES, (pair + 1) * LANES)
            query, key, value = (
                rp[:, c, :, part * INNER + pair * LANES : part * INNER + (pair + 1) * LANES].reshape(total_rows, LANES)
                for part in range(3)
            )
            mixed = []
            for mask in (low, jnp.logical_not(low)):
                scores = lax.dot_general(
                    jnp.where(mask, query, zero), key, (((1,), (1,)), ((), ())), preferred_element_type=f32
                ) * (1.0 / math.sqrt(HEAD))
                scores = jnp.exp(scores - jnp.max(scores, axis=-1, keepdims=True))
                weights = (scores / jnp.sum(scores, axis=-1, keepdims=True)).astype(bf16)
                mixed.append(jnp.dot(weights, value, preferred_element_type=f32))
            ac[:, c, :, span] = jnp.where(low, mixed[0], mixed[1]).astype(bf16).reshape(seqs, rows, LANES)
    exchange(lambda peer: ac.at[peer], ra, 3)
    back = jnp.where((two % rows) * cols + two // rows == one, 1.0, 0.0).astype(bf16)
    arrived(ra, in_seq.at[3])
    result = jnp.dot(back, ra[...].reshape(tokens, INNER), preferred_element_type=f32).astype(bf16)
    cc_ref[...] = result.reshape(rows, cols, INNER)

    sent_head(1, out_k, True)
    sent_head(0, out_q, False)
    sent_head(2, out_v, True)

    @pl.when(worker)
    def _():
        sent(rl, 0)
        sent(rt, 1)
        arrived(oc.at[pl.ds(0, Z - 1)], out_c)

    sent(rp, 2)
    sent(ra, 3)


def body(seqs, alignment, row_gain, row_project, row_output, column_gain, column_project):
    rows, cols, features = alignment.shape
    res = 2 * Z
    here = Z * cols
    share = here // seqs
    per_device = cols // seqs
    bf16 = jnp.bfloat16
    vmem = pl.BlockSpec(memory_space=pltpu.VMEM)
    hbm = pl.BlockSpec(memory_space=pl.ANY)
    head = (rows // 2, cols, LANES)
    dma = pltpu.SemaphoreType.DMA
    return pl.pallas_call(
        functools.partial(kernel, seqs),
        out_shape=(
            jax.ShapeDtypeStruct((rows, cols, features), bf16),
            jax.ShapeDtypeStruct((rows, cols, INNER), bf16),
        ),
        in_specs=[vmem, vmem, vmem, vmem, hbm, hbm],
        out_specs=(vmem, vmem),
        scratch_shapes=[
            pltpu.VMEM(row_output.shape, bf16),
            pltpu.VMEM(column_project.shape, bf16),
            pltpu.VMEM((3, HEADS) + head, bf16),
            pltpu.VMEM((Z,) + head, bf16),
            pltpu.VMEM((res,) + head, bf16),
            pltpu.VMEM((res,) + head, bf16),
            pltpu.VMEM((seqs, 2 * share, here), bf16),
            pltpu.VMEM((seqs, 2 * share, here), bf16),
            pltpu.VMEM((2 * share, here), bf16),
            pltpu.VMEM((seqs, 2 * share, here), bf16),
            pltpu.VMEM((Z,) + head, bf16),
            pltpu.VMEM((HEADS,) + head, bf16),
            pltpu.VMEM((seqs, per_device, rows, 3 * INNER), bf16),
            pltpu.VMEM((seqs, per_device, rows, 3 * INNER), bf16),
            pltpu.VMEM((seqs, per_device, rows, INNER), bf16),
            pltpu.VMEM((seqs, per_device, rows, INNER), bf16),
            dma((2,)),
            dma((HEADS, 1)),
            dma((HEADS, 2)),
            dma((HEADS, 2)),
            dma((3,)),
            dma,
            dma,
            dma((4,)),
            dma((4,)),
        ],
        compiler_params=pltpu.CompilerParams(
            collective_id=0, has_side_effects=True, vmem_limit_bytes=40 * 1024 * 1024
        ),
        name="msa_layer",
    )(
        alignment, row_gain.reshape(1, features), row_project,
        column_gain.reshape(1, features), row_output, column_project,
    )


def solution(mesh):
    placed = (P("seq", "res", None), P(), P(), P(), P(), P())
    return jax.shard_map(
        functools.partial(body, mesh.shape["seq"]),
        mesh=mesh,
        in_specs=placed,
        out_specs=(P("seq", "res", None), P("seq", "res", None)),
        check_vma=False,
    )
```

time: 590 us -> 105 us (0.18)
  waiting for transfers between devices: 495 us -> 0 us
  Pallas kernels: 0 us -> 96 us
  blocking collectives: 38.9 us -> 0 us
  local copies, waits for them, and re-layouts: 22.2 us -> 7.81 us
  between operations: 14 us -> 0.64 us
  matrix products: 12.9 us -> 0 us
  other arithmetic: 6.81 us -> 0 us
    psum x1 -> x0, waiting for transfers between devices: 267 us -> none  [body(): summed = lax.psum(partial_value, 'seq')]
    all_gather x2 -> x0, waiting for transfers between devices: 227 us -> none  [the longest x1 118 us: body(): panel = lax.all_gather(keys_local, 'res', axis=1, tiled=True)]
    pallas_call x0 -> x1, Pallas kernels: none -> 96 us  [body(): pl.pallas_call(functools.partial(kernel, seqs), out_shape=(jax.ShapeDtype...]
    all_to_all x2 -> x0, blocking collectives: 38.9 us -> none  [the longest x1 25.5 us: body(): lax.all_to_all(packed_col, 'seq', split_axis=1, concat_axis=0, tiled=True)]
    dot_general x6 -> x0, matrix products: 11.1 us -> none  [the longest x1 4.31 us: body(): jnp.einsum('hij,rjhe->rihe', tied, panel.reshape(rows_here, panel_cols, H...]
    all_gather x2 -> x0, local copies, waits for them, and re-layouts: 10.1 us -> none  [the longest x1 5.12 us: body(): panel = lax.all_gather(keys_local, 'res', axis=1, tiled=True)]
  transfers between devices with their start and end apart: 3 -> 0, of which waited for: 3 -> 0; matrix products, arithmetic and copies ran while one was open for 2% -> 0% of each run, Pallas kernels for 0% -> 0%
where the time goes in v1:
time: 105 us; the launch traced here: 104 us
  Pallas kernels  96 us (91%)
  local copies, waits for them, and re-layouts  7.81 us (7%)
    pallas_call x1, Pallas kernels, body(): pl.pallas_call(functools.partial(kernel, seqs), out_shape=(jax.ShapeDtype...  96 us
    unnamed x10, local copies, waits for them, and re-layouts  6.44 us

profile of v1, /device:TPU:1, one launch (start us, length us, event | category | flops | bytes accessed | tf_op | source)
XLA Modules:
  0.0 104.5 jit_solution(17401984713666013467)
XLA Ops:
  0.6 0.7 reshape.10.g1_ref
  1.3 0.7 reshape.11.g2_ref
  2.0 0.0 copy-start
  2.0 1.5 %copy-done = bf16[768,1152]{1,0:T(8,128)(2,1)S(1)} copy-done((bf16[768,1152]{1,0:T(8,128)(2,1)S(1)}, bf16[768,1152]{1,0:T(8,128)(2,1)}, u32[]{:S(2)}) %copy-start) | copy-done | bytes 1769496
  3.5 0.0 copy-start.1
  3.5 1.5 %copy-done.1 = bf16[768,1152]{1,0:T(8,128)(2,1)S(1)} copy-done((bf16[768,1152]{1,0:T(8,128)(2,1)S(1)}, bf16[768,1152]{1,0:T(8,128)(2,1)}, u32[]{:S(2)}) %copy-start.1) | copy-done | bytes 1769496
  5.0 0.0 copy-start.2
  5.0 1.1 %copy-done.2 = bf16[384,768]{1,0:T(8,128)(2,1)S(1)} copy-done((bf16[384,768]{1,0:T(8,128)(2,1)S(1)}, bf16[384,768]{1,0:T(8,128)(2,1)}, u32[]{:S(2)}) %copy-start.2) | copy-done | bytes 589848
  6.0 0.0 copy-start.3
  6.0 1.0 copy-done.3
  7.0 96.0 %msa_layer.1 = (bf16[8,32,768]{2,1,0:T(8,128)(2,1)S(1)}, bf16[8,32,384]{2,1,0:T(8,128)(2,1)S(1)}) custom-call(bf16[8,32,768]{2,1,0:T(8,128)(2,1)S(1)} %copy-done.3, bf16[1,768]{1,0:T(2,128)(2,1)S(1)} %reshape.10.g1_ref, bf16[768,1152]{1,0:T(8,128)(2,1)S(1)} %copy-done, bf16[1,768]{1,0:T(2,128)(2,1)S(1)} %reshape.11.g2_ref, bf16[384,768]{1,0:T(8,128)(2,1)S(1)} %copy-done.2, ...), custom_call_target="tpu_custom_call" | custom-call | tf_op jit(solution)/shard_map/msa_layer/pallas_call | solution.py:275
  103.1 0.7 copy.10
  103.8 0.7 copy.11
Async XLA Ops:
  2.0 1.5 %copy-start = (bf16[768,1152]{1,0:T(8,128)(2,1)S(1)}, bf16[768,1152]{1,0:T(8,128)(2,1)}, u32[]{:S(2)}) copy-start(bf16[768,1152]{1,0:T(8,128)(2,1)} %w1_ref.1) | copy-start | bytes 5308420
  3.5 1.5 %copy-start.1 = (bf16[768,1152]{1,0:T(8,128)(2,1)S(1)}, bf16[768,1152]{1,0:T(8,128)(2,1)}, u32[]{:S(2)}) copy-start(bf16[768,1152]{1,0:T(8,128)(2,1)} %w2_hbm.1) | copy-start | bytes 5308420
  5.0 1.1 %copy-start.2 = (bf16[384,768]{1,0:T(8,128)(2,1)S(1)}, bf16[384,768]{1,0:T(8,128)(2,1)}, u32[]{:S(2)}) copy-start(bf16[384,768]{1,0:T(8,128)(2,1)} %wo_hbm.1) | copy-start | bytes 1769476
  6.0 1.0 copy-start.3

commit v2 on v1

v2 whole, which is shorter than its diff:
```python
import functools
import math

import jax
import jax.numpy as jnp
from jax import lax
from jax.experimental import pallas as pl
from jax.experimental.pallas import tpu as pltpu
from jax.sharding import PartitionSpec as P

HEADS = 6
HEAD = 64
INNER = HEADS * HEAD
LANES = 128
Z = 8
CORES = 2
FAR_FIRST = (4, 3, 5, 2, 6, 1, 7, 0)
MESH = pl.DeviceIdType.MESH


def layer_norm(values, gain):
    average = jnp.mean(values, axis=-1, keepdims=True)
    centred = values - average
    spread = jnp.mean(centred * centred, axis=-1, keepdims=True)
    return centred * lax.rsqrt(spread + 1e-05) * gain.astype(jnp.float32)


def low_lanes(shape):
    return lax.broadcasted_iota(jnp.int32, shape, len(shape) - 1) < HEAD


def arrived(ref, sem):
    pltpu.make_async_copy(ref, ref, sem).wait()


def kernel(
    seqs, x_hbm, g1_ref, w1_hbm, g2_ref, wo_hbm, w2_hbm, ru_ref, cc_ref,
    x_ref, w1_ref, wo_ref, w2_ref, tiles, rq, rk, rv, lp, rl, l2, r2, td, rd, t4, rt, oc, rc,
    xs, rx, cs, rcs, ac, ra,
    load_sem, out_q, out_k, out_v, in_q, in_k, in_v, out_c, in_c, out_seq, in_seq,
):
    rows, cols, features = x_ref.shape
    tokens = rows * cols
    half = tokens // 2
    quads = rows // 2
    res = 2 * Z
    here = Z * cols
    everywhere = res * cols
    per_device = cols // seqs
    n_b = min(4, seqs // CORES)
    n_a = seqs // n_b
    f32, bf16 = jnp.float32, jnp.bfloat16

    s = lax.axis_index("seq")
    t = lax.axis_index("res")
    yh = t // Z
    z = t % Z
    worker = z % 4 != 3
    head_here = z - z // 4
    core = s % CORES
    b = (s // CORES) % n_b
    a = s // (CORES * n_b) * CORES + core

    def a_peer(k):
        return (k // CORES) * (CORES * n_b) + b * CORES + k % CORES

    def b_peer(k):
        return (a // CORES) * (CORES * n_b) + k * CORES + core

    def s_peer(k):
        return k

    loads = [
        pltpu.make_async_copy(src, dst, load_sem.at[i])
        for i, (src, dst) in enumerate(
            ((x_hbm, x_ref), (w1_hbm, w1_ref), (wo_hbm, wo_ref), (w2_hbm, w2_ref))
        )
    ]
    for load in loads:
        load.start()

    barrier = pltpu.get_barrier_semaphore()

    def greet_seq(k, carry):
        pl.semaphore_signal(barrier, inc=1, device_id={"seq": lax.rem(s + k, seqs)}, device_id_type=MESH)
        return carry

    def greet_res(k, carry):
        pl.semaphore_signal(barrier, inc=1, device_id={"res": lax.rem(t + k, res)}, device_id_type=MESH)
        return carry

    lax.fori_loop(1, res, greet_res, 0)
    lax.fori_loop(1, seqs, greet_seq, 0)

    loads[0].wait()
    source = x_ref[...].reshape(tokens, features).astype(f32)
    normed = layer_norm(source, g1_ref[...].reshape(1, features)).astype(bf16)
    loads[1].wait()

    def project(part):
        packed = jnp.dot(normed, w1_ref[:, part * INNER : (part + 1) * INNER], preferred_element_type=f32)
        for pair in range(HEADS // 2):
            tile = packed[:, pair * LANES : (pair + 1) * LANES]
            turned = pltpu.roll(tile, HEAD, 1)
            low = low_lanes((half, LANES))
            first = jnp.where(low, tile[:half], turned[half:]).astype(bf16)
            second = jnp.where(low, turned[:half], tile[half:]).astype(bf16)
            tiles[part, 2 * pair] = first.reshape(quads, cols, LANES)
            tiles[part, 2 * pair + 1] = second.reshape(quads, cols, LANES)

    def send_head(part, dst, slot, send, recv, both, offsets=FAR_FIRST):
        for offset in offsets:
            at = lax.rem(z + offset, Z)

            @pl.when(at % 4 != 3)
            def _():
                h = at - at // 4
                block = tiles.at[part, h]
                if offset == 0:
                    pltpu.make_async_copy(block, dst.at[slot], recv).start()
                else:
                    pltpu.make_async_remote_copy(
                        block, dst.at[slot], send.at[h, 0], recv,
                        device_id={"res": yh * Z + at}, device_id_type=MESH,
                    ).start()
                if both:
                    pltpu.make_async_remote_copy(
                        block, dst.at[slot], send.at[h, 1], recv,
                        device_id={"res": (1 - yh) * Z + at}, device_id_type=MESH,
                    ).start()

    def sent_head(part, send, both):
        def step(h, carry):
            at = h + h // 3
            block = tiles.at[part, h]

            @pl.when(z != at)
            def _():
                arrived(block, send.at[h, 0])

            if both:
                arrived(block, send.at[h, 1])
            return carry

        lax.fori_loop(0, HEADS, step, 0)

    def exchange(block, dst, stage, me, count, peer_of):
        pltpu.make_async_copy(block(me), dst.at[me], in_seq.at[stage]).start()

        def step(k, carry):
            peer = lax.rem(me + k, count)
            pltpu.make_async_remote_copy(
                block(peer), dst.at[me], out_seq.at[stage], in_seq.at[stage],
                device_id={"seq": peer_of(peer)}, device_id_type=MESH,
            ).start()
            return carry

        lax.fori_loop(1, count, step, 0)

    def sent(dst, stage, count):
        arrived(dst.at[pl.ds(0, count - 1)], out_seq.at[stage])

    project(1)
    pl.semaphore_wait(barrier, seqs + res - 2)
    send_head(1, rk, t, out_k, in_k, True)
    project(0)
    send_head(0, rq, z, out_q, in_q, False)
    project(2)

    @pl.when(jnp.logical_not(worker))
    def _():
        send_head(2, rv, t, out_v, in_v, True)

    one = lax.broadcasted_iota(jnp.int32, (tokens, tokens), 0)
    two = lax.broadcasted_iota(jnp.int32, (tokens, tokens), 1)
    turn = jnp.where((one % rows) * cols + one // rows == two, 1.0, 0.0).astype(bf16)
    back = jnp.where((two % rows) * cols + two // rows == one, 1.0, 0.0).astype(bf16)
    turned = jnp.dot(turn, x_ref[...].reshape(tokens, features), preferred_element_type=f32)
    xs[...] = turned.astype(bf16).reshape(seqs, per_device, rows, features)

    @pl.when(worker)
    def _():
        arrived(rk, in_k)
        arrived(rq, in_q)
        queries = jnp.concatenate([rq[:, r].reshape(here, LANES) for r in range(quads)], axis=1)
        keys = jnp.concatenate([rk[:, r].reshape(everywhere, LANES) for r in range(quads)], axis=1)
        logits = lax.dot_general(
            queries, keys, (((1,), (1,)), ((), ())), preferred_element_type=f32
        ) * (1.0 / (math.sqrt(HEAD) * math.sqrt(rows * seqs)))
        lp[...] = logits.astype(bf16).reshape(n_a, here // n_a, everywhere)
        exchange(lambda peer: lp.at[peer], rl, 0, a, n_a, a_peer)
        send_head(2, rv, t, out_v, in_v, True, FAR_FIRST[:2])
        arrived(rl, in_seq.at[0])
        total = jnp.sum(rl[...].astype(f32), axis=0)
        l2[...] = total.reshape(n_b, here // seqs, everywhere)
        exchange(lambda peer: l2.at[peer], r2, 1, b, n_b, b_peer)
        send_head(2, rv, t, out_v, in_v, True, FAR_FIRST[2:4])
        arrived(r2, in_seq.at[1])
        total = jnp.sum(r2[...], axis=0)
        total = jnp.exp(total - jnp.max(total, axis=-1, keepdims=True))
        total = total / jnp.sum(total, axis=-1, keepdims=True)
        td[...] = jnp.concatenate([total[:, :here], total[:, here:]], axis=0).astype(bf16)
        exchange(lambda peer: td, rd, 2, b, n_b, b_peer)
        send_head(2, rv, t, out_v, in_v, True, FAR_FIRST[4:6])
        arrived(rd, in_seq.at[2])
        tied = rd[...].astype(f32)
        tied = jnp.concatenate([tied[:, : here // seqs], tied[:, here // seqs :]], axis=2)
        t4[...] = tied.reshape(here // n_a, everywhere).astype(bf16)
        exchange(lambda peer: t4, rt, 3, a, n_a, a_peer)
        send_head(2, rv, t, out_v, in_v, True, FAR_FIRST[6:])
        arrived(rv, in_v)
        values = jnp.concatenate([rv[:, r].reshape(everywhere, LANES) for r in range(quads)], axis=1)
        arrived(rt, in_seq.at[3])
        context = jnp.dot(rt[...].reshape(here, everywhere), values, preferred_element_type=f32)
        for r in range(quads):
            oc[:, r] = context[:, r * LANES : (r + 1) * LANES].reshape(Z, cols, LANES).astype(bf16)
        for offset in FAR_FIRST:
            peer = lax.rem(z + offset, Z)
            if offset == 0:
                pltpu.make_async_copy(oc.at[z], rc.at[head_here], in_c).start()
            else:
                pltpu.make_async_remote_copy(
                    oc.at[peer], rc.at[head_here], out_c, in_c,
                    device_id={"res": yh * Z + peer}, device_id_type=MESH,
                ).start()

    exchange(lambda peer: xs.at[peer], rx, 4, s, seqs, s_peer)
    arrived(rc, in_c)
    low = low_lanes((half, LANES))
    tops, bottoms = [], []
    for pair in range(HEADS // 2):
        first = rc[2 * pair].reshape(half, LANES).astype(f32)
        second = rc[2 * pair + 1].reshape(half, LANES).astype(f32)
        tops.append(jnp.where(low, first, pltpu.roll(second, HEAD, 1)).astype(bf16))
        bottoms.append(jnp.where(low, pltpu.roll(first, HEAD, 1), second).astype(bf16))
    context = jnp.concatenate(
        [jnp.concatenate(tops, axis=1), jnp.concatenate(bottoms, axis=1)], axis=0
    )
    turned = jnp.dot(turn, context, preferred_element_type=f32)
    cs[...] = turned.astype(bf16).reshape(seqs, per_device, rows, INNER)
    exchange(lambda peer: cs.at[peer], rcs, 5, s, seqs, s_peer)
    loads[2].wait()
    loads[3].wait()

    update = jnp.dot(context, wo_ref[...], preferred_element_type=f32)
    source = x_ref[...].reshape(tokens, features).astype(f32)
    ru_ref[...] = (source + update).astype(bf16).reshape(rows, cols, features)
    arrived(rx, in_seq.at[4])
    arrived(rcs, in_seq.at[5])

    total_rows = seqs * rows
    low = low_lanes((total_rows, LANES))
    zero = jnp.zeros((total_rows, LANES), bf16)
    for c in range(per_device):
        update = jnp.dot(rcs[:, c].reshape(total_rows, INNER), wo_ref[...], preferred_element_type=f32)
        updated = (rx[:, c].reshape(total_rows, features).astype(f32) + update).astype(bf16)
        normed = layer_norm(updated.astype(f32), g2_ref[...].reshape(1, features)).astype(bf16)
        packed = jnp.dot(normed, w2_ref[...], preferred_element_type=f32).astype(bf16)
        for pair in range(HEADS // 2):
            span = slice(pair * LANES, (pair + 1) * LANES)
            query, key, value = (
                packed[:, part * INNER + pair * LANES : part * INNER + (pair + 1) * LANES]
                for part in range(3)
            )
            mixed = []
            for mask in (low, jnp.logical_not(low)):
                scores = lax.dot_general(
                    jnp.where(mask, query, zero), key, (((1,), (1,)), ((), ())), preferred_element_type=f32
                ) * (1.0 / math.sqrt(HEAD))
                scores = jnp.exp(scores - jnp.max(scores, axis=-1, keepdims=True))
                weights = (scores / jnp.sum(scores, axis=-1, keepdims=True)).astype(bf16)
                mixed.append(jnp.dot(weights, value, preferred_element_type=f32))
            ac[:, c, :, span] = jnp.where(low, mixed[0], mixed[1]).astype(bf16).reshape(seqs, rows, LANES)
    exchange(lambda peer: ac.at[peer], ra, 6, s, seqs, s_peer)
    sent_head(1, out_k, True)
    sent_head(0, out_q, False)
    sent_head(2, out_v, True)

    @pl.when(worker)
    def _():
        sent(rl, 0, n_a)
        sent(r2, 1, n_b)
        sent(rd, 2, n_b)
        sent(rt, 3, n_a)
        arrived(oc.at[pl.ds(0, Z - 1)], out_c)

    sent(rx, 4, seqs)
    sent(rcs, 5, seqs)
    arrived(ra, in_seq.at[6])
    result = jnp.dot(back, ra[...].reshape(tokens, INNER), preferred_element_type=f32).astype(bf16)
    cc_ref[...] = result.reshape(rows, cols, INNER)
    sent(ra, 6, seqs)


def body(seqs, alignment, row_gain, row_project, row_output, column_gain, column_project):
    rows, cols, features = alignment.shape
    res = 2 * Z
    here = Z * cols
    everywhere = res * cols
    share = here // seqs
    per_device = cols // seqs
    n_b = min(4, seqs // CORES)
    n_a = seqs // n_b
    f32, bf16 = jnp.float32, jnp.bfloat16
    vmem = pl.BlockSpec(memory_space=pltpu.VMEM)
    hbm = pl.BlockSpec(memory_space=pl.ANY)
    head = (rows // 2, cols, LANES)
    dma = pltpu.SemaphoreType.DMA
    return pl.pallas_call(
        functools.partial(kernel, seqs),
        out_shape=(
            jax.ShapeDtypeStruct((rows, cols, features), bf16),
            jax.ShapeDtypeStruct((rows, cols, INNER), bf16),
        ),
        in_specs=[hbm, vmem, hbm, vmem, hbm, hbm],
        out_specs=(vmem, vmem),
        scratch_shapes=[
            pltpu.VMEM(alignment.shape, bf16),
            pltpu.VMEM(row_project.shape, bf16),
            pltpu.VMEM(row_output.shape, bf16),
            pltpu.VMEM(column_project.shape, bf16),
            pltpu.VMEM((3, HEADS) + head, bf16),
            pltpu.VMEM((Z,) + head, bf16),
            pltpu.VMEM((res,) + head, bf16),
            pltpu.VMEM((res,) + head, bf16),
            pltpu.VMEM((n_a, here // n_a, everywhere), bf16),
            pltpu.VMEM((n_a, here // n_a, everywhere), bf16),
            pltpu.VMEM((n_b, share, everywhere), f32),
            pltpu.VMEM((n_b, share, everywhere), f32),
            pltpu.VMEM((2 * share, here), bf16),
            pltpu.VMEM((n_b, 2 * share, here), bf16),
            pltpu.VMEM((here // n_a, everywhere), bf16),
            pltpu.VMEM((n_a, here // n_a, everywhere), bf16),
            pltpu.VMEM((Z,) + head, bf16),
            pltpu.VMEM((HEADS,) + head, bf16),
            pltpu.VMEM((seqs, per_device, rows, features), bf16),
            pltpu.VMEM((seqs, per_device, rows, features), bf16),
            pltpu.VMEM((seqs, per_device, rows, INNER), bf16),
            pltpu.VMEM((seqs, per_device, rows, INNER), bf16),
            pltpu.VMEM((seqs, per_device, rows, INNER), bf16),
            pltpu.VMEM((seqs, per_device, rows, INNER), bf16),
            dma((4,)),
            dma((HEADS, 1)),
            dma((HEADS, 2)),
            dma((HEADS, 2)),
            dma,
            dma,
            dma,
            dma,
            dma,
            dma((7,)),
            dma((7,)),
        ],
        compiler_params=pltpu.CompilerParams(
            collective_id=0, has_side_effects=True, vmem_limit_bytes=60 * 1024 * 1024
        ),
        name="msa_layer",
    )(
        alignment, row_gain, row_project, column_gain, row_output, column_project,
    )


def solution(mesh):
    placed = (P("seq", "res", None), P(), P(), P(), P(), P())
    return jax.shard_map(
        functools.partial(body, mesh.shape["seq"]),
        mesh=mesh,
        in_specs=placed,
        out_specs=(P("seq", "res", None), P("seq", "res", None)),
        check_vma=False,
    )
```

time: 105 us -> 88.9 us (0.85)
  Pallas kernels: 96 us -> 84.6 us
  local copies, waits for them, and re-layouts: 7.81 us -> 3.39 us
    pallas_call x1, Pallas kernels: 96 us -> 84.6 us  [body(): pl.pallas_call(functools.partial(kernel, seqs), out_shape=(jax.ShapeDtype...]
    unnamed x10 -> x2, local copies, waits for them, and re-layouts: 6.44 us -> 3.39 us
    reshape x2 -> x0, local copies, waits for them, and re-layouts: 1.37 us -> none  [the longest x1 0.69 us: body(): row_gain.reshape(1, features)]
where the time goes in v2:
time: 88.9 us; the launch traced here: 88.7 us
  Pallas kernels  84.6 us (95%)
  local copies, waits for them, and re-layouts  3.39 us (4%)
    pallas_call x1, Pallas kernels, body(): pl.pallas_call(functools.partial(kernel, seqs), out_shape=(jax.ShapeDtype...  84.6 us
    unnamed x2, local copies, waits for them, and re-layouts  3.39 us

profile of v2, /device:TPU:1, one launch (start us, length us, event | category | flops | bytes accessed | tf_op | source)
XLA Modules:
  0.0 88.7 jit_solution(15168692985718873459)
XLA Ops:
  0.6 84.6 %msa_layer.1 = (bf16[8,32,768]{2,1,0:T(8,128)(2,1)}, bf16[8,32,384]{2,1,0:T(8,128)(2,1)}) custom-call(bf16[8,32,768]{2,1,0:T(8,128)(2,1)} %x_hbm.1, bf16[768]{0:T(1024)(128)(2,1)} %g1_ref.1, bf16[768,1152]{1,0:T(8,128)(2,1)} %w1_hbm.1, bf16[768]{0:T(1024)(128)(2,1)} %g2_ref.1, bf16[384,768]{1,0:T(8,128)(2,1)} %wo_hbm.1, bf16[768,1152]{1,0:T(8,128)(2,1)} %w2_hbm.1), custom_call_target="tpu_custom_call" | custom-call | tf_op jit(solution)/shard_map/msa_layer/pallas_call | solution.py:309
  85.3 1.8 %copy.10 = bf16[8,32,768]{2,1,0:T(8,128)(2,1)} copy(bf16[8,32,768]{2,1,0:T(8,128)(2,1)} %get-tuple-element.4) | data formatting | bytes 786432
  87.0 1.6 %copy.11 = bf16[8,32,384]{2,1,0:T(8,128)(2,1)} copy(bf16[8,32,384]{2,1,0:T(8,128)(2,1)} %get-tuple-element.5) | data formatting | bytes 393216

commit v3 on v2

--- a/solution.py
+++ b/solution.py
@@ -34,10 +34,10 @@
 
 
 def kernel(
-    seqs, x_hbm, g1_ref, w1_hbm, g2_ref, wo_hbm, w2_hbm, ru_ref, cc_ref,
-    x_ref, w1_ref, wo_ref, w2_ref, tiles, rq, rk, rv, lp, rl, l2, r2, td, rd, t4, rt, oc, rc,
+    seqs, x_hbm, g1_hbm, w1_hbm, g2_hbm, wo_hbm, w2_hbm, ru_ref, cc_ref,
+    x_ref, g1_ref, w1_ref, g2_ref, wo_ref, w2_ref, tiles, rq, rk, rv, lp, rl, l2, r2, t4, rt, oc, rc,
     xs, rx, cs, rcs, ac, ra,
-    load_sem, out_q, out_k, out_v, in_q, in_k, in_v, out_c, in_c, out_seq, in_seq,
+    load_sem, out_q, out_k, out_v, out_p, in_p, in_q, in_k, in_v, out_c, in_c, out_seq, in_seq,
 ):
     rows, cols, features = x_ref.shape
     tokens = rows * cols
@@ -61,6 +61,9 @@
     b = (s // CORES) % n_b
     a = s // (CORES * n_b) * CORES + core
 
+    def away(offset):
+        return lax.rem(z + offset + core * (Z - 2 * offset), Z)
+
     def a_peer(k):
         return (k // CORES) * (CORES * n_b) + b * CORES + k % CORES
 
@@ -73,7 +76,10 @@
     loads = [
         pltpu.make_async_copy(src, dst, load_sem.at[i])
         for i, (src, dst) in enumerate(
-            ((x_hbm, x_ref), (w1_hbm, w1_ref), (wo_hbm, wo_ref), (w2_hbm, w2_ref))
+            (
+                (x_hbm, x_ref), (g1_hbm, g1_ref), (w1_hbm, w1_ref),
+                (g2_hbm, g2_ref), (wo_hbm, wo_ref), (w2_hbm, w2_ref),
+            )
         )
     ]
     for load in loads:
@@ -93,9 +99,10 @@
     lax.fori_loop(1, seqs, greet_seq, 0)
 
     loads[0].wait()
+    loads[1].wait()
     source = x_ref[...].reshape(tokens, features).astype(f32)
     normed = layer_norm(source, g1_ref[...].reshape(1, features)).astype(bf16)
-    loads[1].wait()
+    loads[2].wait()
 
     def project(part):
         packed = jnp.dot(normed, w1_ref[:, part * INNER : (part + 1) * INNER], preferred_element_type=f32)
@@ -110,7 +117,7 @@
 
     def send_head(part, dst, slot, send, recv, both, offsets=FAR_FIRST):
         for offset in offsets:
-            at = lax.rem(z + offset, Z)
+            at = away(offset)
 
             @pl.when(at % 4 != 3)
             def _():
@@ -129,6 +136,12 @@
                         device_id={"res": (1 - yh) * Z + at}, device_id_type=MESH,
                     ).start()
 
+    def send_values(offsets):
+        if offsets[0] == FAR_FIRST[0]:
+            pass_values.wait_recv()
+        send_head(2, rv, t, out_v.at[0], in_v, False, offsets)
+        send_head(3, rv, (1 - yh) * Z + z, out_v.at[1], in_v, False, offsets)
+
     def sent_head(part, send, both):
         def step(h, carry):
             at = h + h // 3
@@ -148,7 +161,7 @@
         pltpu.make_async_copy(block(me), dst.at[me], in_seq.at[stage]).start()
 
         def step(k, carry):
-            peer = lax.rem(me + k, count)
+            peer = lax.rem(me + k + core * (count - 2 * k), count)
             pltpu.make_async_remote_copy(
                 block(peer), dst.at[me], out_seq.at[stage], in_seq.at[stage],
                 device_id={"seq": peer_of(peer)}, device_id_type=MESH,
@@ -167,9 +180,14 @@
     send_head(0, rq, z, out_q, in_q, False)
     project(2)
 
+    pass_values = pltpu.make_async_remote_copy(
+        tiles.at[2], tiles.at[3], out_p, in_p, device_id={"res": (1 - yh) * Z + z}, device_id_type=MESH
+    )
+    pass_values.start()
+
     @pl.when(jnp.logical_not(worker))
     def _():
-        send_head(2, rv, t, out_v, in_v, True)
+        send_values(FAR_FIRST)
 
     one = lax.broadcasted_iota(jnp.int32, (tokens, tokens), 0)
     two = lax.broadcasted_iota(jnp.int32, (tokens, tokens), 1)
@@ -189,33 +207,27 @@
         ) * (1.0 / (math.sqrt(HEAD) * math.sqrt(rows * seqs)))
         lp[...] = logits.astype(bf16).reshape(n_a, here // n_a, everywhere)
         exchange(lambda peer: lp.at[peer], rl, 0, a, n_a, a_peer)
-        send_head(2, rv, t, out_v, in_v, True, FAR_FIRST[:2])
+        send_values(FAR_FIRST[:3])
         arrived(rl, in_seq.at[0])
         total = jnp.sum(rl[...].astype(f32), axis=0)
-        l2[...] = total.reshape(n_b, here // seqs, everywhere)
-        exchange(lambda peer: l2.at[peer], r2, 1, b, n_b, b_peer)
-        send_head(2, rv, t, out_v, in_v, True, FAR_FIRST[2:4])
+        l2[...] = total.astype(bf16)
+        exchange(lambda peer: l2, r2, 1, b, n_b, b_peer)
+        send_values(FAR_FIRST[3:6])
         arrived(r2, in_seq.at[1])
-        total = jnp.sum(r2[...], axis=0)
+        total = jnp.sum(r2[...].astype(f32), axis=0)
         total = jnp.exp(total - jnp.max(total, axis=-1, keepdims=True))
         total = total / jnp.sum(total, axis=-1, keepdims=True)
-        td[...] = jnp.concatenate([total[:, :here], total[:, here:]], axis=0).astype(bf16)
-        exchange(lambda peer: td, rd, 2, b, n_b, b_peer)
-        send_head(2, rv, t, out_v, in_v, True, FAR_FIRST[4:6])
-        arrived(rd, in_seq.at[2])
-        tied = rd[...].astype(f32)
-        tied = jnp.concatenate([tied[:, : here // seqs], tied[:, here // seqs :]], axis=2)
-        t4[...] = tied.reshape(here // n_a, everywhere).astype(bf16)
-        exchange(lambda peer: t4, rt, 3, a, n_a, a_peer)
-        send_head(2, rv, t, out_v, in_v, True, FAR_FIRST[6:])
+        t4[...] = total.astype(bf16)
+        exchange(lambda peer: t4, rt, 2, a, n_a, a_peer)
+        send_values(FAR_FIRST[6:])
         arrived(rv, in_v)
         values = jnp.concatenate([rv[:, r].reshape(everywhere, LANES) for r in range(quads)], axis=1)
-        arrived(rt, in_seq.at[3])
+        arrived(rt, in_seq.at[2])
         context = jnp.dot(rt[...].reshape(here, everywhere), values, preferred_element_type=f32)
         for r in range(quads):
             oc[:, r] = context[:, r * LANES : (r + 1) * LANES].reshape(Z, cols, LANES).astype(bf16)
         for offset in FAR_FIRST:
-            peer = lax.rem(z + offset, Z)
+            peer = away(offset)
             if offset == 0:
                 pltpu.make_async_copy(oc.at[z], rc.at[head_here], in_c).start()
             else:
@@ -224,7 +236,7 @@
                     device_id={"res": yh * Z + peer}, device_id_type=MESH,
                 ).start()
 
-    exchange(lambda peer: xs.at[peer], rx, 4, s, seqs, s_peer)
+    exchange(lambda peer: xs.at[peer], rx, 3, s, seqs, s_peer)
     arrived(rc, in_c)
     low = low_lanes((half, LANES))
     tops, bottoms = [], []
@@ -238,15 +250,15 @@
     )
     turned = jnp.dot(turn, context, preferred_element_type=f32)
     cs[...] = turned.astype(bf16).reshape(seqs, per_device, rows, INNER)
-    exchange(lambda peer: cs.at[peer], rcs, 5, s, seqs, s_peer)
-    loads[2].wait()
-    loads[3].wait()
+    exchange(lambda peer: cs.at[peer], rcs, 4, s, seqs, s_peer)
+    for load in loads[3:]:
+        load.wait()
 
     update = jnp.dot(context, wo_ref[...], preferred_element_type=f32)
     source = x_ref[...].reshape(tokens, features).astype(f32)
     ru_ref[...] = (source + update).astype(bf16).reshape(rows, cols, features)
-    arrived(rx, in_seq.at[4])
-    arrived(rcs, in_seq.at[5])
+    arrived(rx, in_seq.at[3])
+    arrived(rcs, in_seq.at[4])
 
     total_rows = seqs * rows
     low = low_lanes((total_rows, LANES))
@@ -271,25 +283,26 @@
                 weights = (scores / jnp.sum(scores, axis=-1, keepdims=True)).astype(bf16)
                 mixed.append(jnp.dot(weights, value, preferred_element_type=f32))
             ac[:, c, :, span] = jnp.where(low, mixed[0], mixed[1]).astype(bf16).reshape(seqs, rows, LANES)
-    exchange(lambda peer: ac.at[peer], ra, 6, s, seqs, s_peer)
+    exchange(lambda peer: ac.at[peer], ra, 5, s, seqs, s_peer)
     sent_head(1, out_k, True)
     sent_head(0, out_q, False)
-    sent_head(2, out_v, True)
+    sent_head(2, out_v.at[0], False)
+    sent_head(3, out_v.at[1], False)
+    pass_values.wait_send()
 
     @pl.when(worker)
     def _():
         sent(rl, 0, n_a)
         sent(r2, 1, n_b)
-        sent(rd, 2, n_b)
-        sent(rt, 3, n_a)
+        sent(rt, 2, n_a)
         arrived(oc.at[pl.ds(0, Z - 1)], out_c)
 
-    sent(rx, 4, seqs)
-    sent(rcs, 5, seqs)
-    arrived(ra, in_seq.at[6])
+    sent(rx, 3, seqs)
+    sent(rcs, 4, seqs)
+    arrived(ra, in_seq.at[5])
     result = jnp.dot(back, ra[...].reshape(tokens, INNER), preferred_element_type=f32).astype(bf16)
     cc_ref[...] = result.reshape(rows, cols, INNER)
-    sent(ra, 6, seqs)
+    sent(ra, 5, seqs)
 
 
 def body(seqs, alignment, row_gain, row_project, row_output, column_gain, column_project):
@@ -297,13 +310,13 @@
     res = 2 * Z
     here = Z * cols
     everywhere = res * cols
-    share = here // seqs
     per_device = cols // seqs
     n_b = min(4, seqs // CORES)
     n_a = seqs // n_b
-    f32, bf16 = jnp.float32, jnp.bfloat16
+    bf16 = jnp.bfloat16
     vmem = pl.BlockSpec(memory_space=pltpu.VMEM)
-    hbm = pl.BlockSpec(memory_space=pl.ANY)
+    far = functools.partial(pltpu.with_memory_space_constraint, memory_space=pltpu.HBM)
+    hbm = pl.BlockSpec(memory_space=pltpu.HBM)
     head = (rows // 2, cols, LANES)
     dma = pltpu.SemaphoreType.DMA
     return pl.pallas_call(
@@ -312,23 +325,23 @@
             jax.ShapeDtypeStruct((rows, cols, features), bf16),
             jax.ShapeDtypeStruct((rows, cols, INNER), bf16),
         ),
-        in_specs=[hbm, vmem, hbm, vmem, hbm, hbm],
+        in_specs=[hbm] * 6,
         out_specs=(vmem, vmem),
         scratch_shapes=[
-            pltpu.VMEM(alignment.shape, bf16),
-            pltpu.VMEM(row_project.shape, bf16),
-            pltpu.VMEM(row_output.shape, bf16),
-            pltpu.VMEM(column_project.shape, bf16),
-            pltpu.VMEM((3, HEADS) + head, bf16),
+            *(
+                pltpu.VMEM(operand.shape, bf16)
+                for operand in (
+                    alignment, row_gain, row_project, column_gain, row_output, column_project
+                )
+            ),
+            pltpu.VMEM((4, HEADS) + head, bf16),
             pltpu.VMEM((Z,) + head, bf16),
             pltpu.VMEM((res,) + head, bf16),
             pltpu.VMEM((res,) + head, bf16),
             pltpu.VMEM((n_a, here // n_a, everywhere), bf16),
             pltpu.VMEM((n_a, here // n_a, everywhere), bf16),
-            pltpu.VMEM((n_b, share, everywhere), f32),
-            pltpu.VMEM((n_b, share, everywhere), f32),
-            pltpu.VMEM((2 * share, here), bf16),
-            pltpu.VMEM((n_b, 2 * share, here), bf16),
+            pltpu.VMEM((here // n_a, everywhere), bf16),
+            pltpu.VMEM((n_b, here // n_a, everywhere), bf16),
             pltpu.VMEM((here // n_a, everywhere), bf16),
             pltpu.VMEM((n_a, here // n_a, everywhere), bf16),
             pltpu.VMEM((Z,) + head, bf16),
@@ -339,24 +352,26 @@
             pltpu.VMEM((seqs, per_device, rows, INNER), bf16),
             pltpu.VMEM((seqs, per_device, rows, INNER), bf16),
             pltpu.VMEM((seqs, per_device, rows, INNER), bf16),
-            dma((4,)),
+            dma((6,)),
             dma((HEADS, 1)),
             dma((HEADS, 2)),
-            dma((HEADS, 2)),
-            dma,
-            dma,
-            dma,
-            dma,
-            dma,
-            dma((7,)),
-            dma((7,)),
+            dma((2, HEADS, 1)),
+            dma,
+            dma,
+            dma,
+            dma,
+            dma,
+            dma,
+            dma,
+            dma((6,)),
+            dma((6,)),
         ],
         compiler_params=pltpu.CompilerParams(
-            collective_id=0, has_side_effects=True, vmem_limit_bytes=60 * 1024 * 1024
+            collective_id=0, has_side_effects=True, vmem_limit_bytes=40 * 1024 * 1024
         ),
         name="msa_layer",
     )(
-        alignment, row_gain, row_project, column_gain, row_output, column_project,
+        far(alignment), far(row_gain), far(row_project), far(column_gain), far(row_output), far(column_project),
     )
 
 

time: 88.9 us -> 78.8 us (0.89)
  Pallas kernels: 84.6 us -> 76.6 us
  local copies, waits for them, and re-layouts: 3.39 us -> 1.42 us
    pallas_call x1, Pallas kernels: 84.6 us -> 76.6 us  [body(): pl.pallas_call(functools.partial(kernel, seqs), out_shape=(jax.ShapeDtype...]
    unnamed x2, local copies, waits for them, and re-layouts: 3.39 us -> 1.42 us
where the time goes in v3:
time: 78.8 us; the launch traced here: 78.7 us
  Pallas kernels  76.6 us (97%)
  local copies, waits for them, and re-layouts  1.42 us (2%)
    pallas_call x1, Pallas kernels, body(): pl.pallas_call(functools.partial(kernel, seqs), out_shape=(jax.ShapeDtype...  76.6 us

profile of v3, /device:TPU:1, one launch (start us, length us, event | category | flops | bytes accessed | tf_op | source)
XLA Modules:
  0.0 78.7 jit_solution(12405650401015211590)
XLA Ops:
  0.6 76.6 %msa_layer.1 = (bf16[8,32,768]{2,1,0:T(8,128)(2,1)S(1)}, bf16[8,32,384]{2,1,0:T(8,128)(2,1)S(1)}) custom-call(bf16[8,32,768]{2,1,0:T(8,128)(2,1)} %x_hbm.1, bf16[768]{0:T(1024)(128)(2,1)} %g1_hbm.1, bf16[768,1152]{1,0:T(8,128)(2,1)} %w1_hbm.1, bf16[768]{0:T(1024)(128)(2,1)} %g2_hbm.1, bf16[384,768]{1,0:T(8,128)(2,1)} %wo_hbm.1, bf16[768,1152]{1,0:T(8,128)(2,1)} %w2_hbm.1), custom_call_target="tpu_custom_call" | custom-call | tf_op jit(solution)/shard_map/msa_layer/pallas_call | solution.py:322
  77.3 0.7 copy.10
  78.0 0.7 copy.11

commit v4 on v3

--- a/solution.py
+++ b/solution.py
@@ -37,7 +37,7 @@
     seqs, x_hbm, g1_hbm, w1_hbm, g2_hbm, wo_hbm, w2_hbm, ru_ref, cc_ref,
     x_ref, g1_ref, w1_ref, g2_ref, wo_ref, w2_ref, tiles, rq, rk, rv, lp, rl, l2, r2, t4, rt, oc, rc,
     xs, rx, cs, rcs, ac, ra,
-    load_sem, out_q, out_k, out_v, out_p, in_p, in_q, in_k, in_v, out_c, in_c, out_seq, in_seq,
+    load_sem, out_q, out_k, out_v, out_p, in_p, in_q, in_k, in_v, out_c, in_c, out_t, in_t, out_seq, in_seq,
 ):
     rows, cols, features = x_ref.shape
     tokens = rows * cols
@@ -49,6 +49,7 @@
     per_device = cols // seqs
     n_b = min(4, seqs // CORES)
     n_a = seqs // n_b
+    count_t = Z // n_a
     f32, bf16 = jnp.float32, jnp.bfloat16
 
     s = lax.axis_index("seq")
@@ -177,7 +178,7 @@
     pl.semaphore_wait(barrier, seqs + res - 2)
     send_head(1, rk, t, out_k, in_k, True)
     project(0)
-    send_head(0, rq, z, out_q, in_q, False)
+    send_head(0, rq, z, out_q, in_q.at[z], False)
     project(2)
 
     pass_values = pltpu.make_async_remote_copy(
@@ -199,14 +200,29 @@
     @pl.when(worker)
     def _():
         arrived(rk, in_k)
-        arrived(rq, in_q)
-        queries = jnp.concatenate([rq[:, r].reshape(here, LANES) for r in range(quads)], axis=1)
         keys = jnp.concatenate([rk[:, r].reshape(everywhere, LANES) for r in range(quads)], axis=1)
-        logits = lax.dot_general(
-            queries, keys, (((1,), (1,)), ((), ())), preferred_element_type=f32
-        ) * (1.0 / (math.sqrt(HEAD) * math.sqrt(rows * seqs)))
-        lp[...] = logits.astype(bf16).reshape(n_a, here // n_a, everywhere)
-        exchange(lambda peer: lp.at[peer], rl, 0, a, n_a, a_peer)
+        for offset in (4, 5, 3, 6, 2, 7, 1, 0):
+            origin = away(offset)
+            arrived(rq.at[origin], in_q.at[origin])
+            queries = jnp.concatenate([rq[origin, r] for r in range(quads)], axis=1)
+            logits = lax.dot_general(
+                queries, keys, (((1,), (1,)), ((), ())), preferred_element_type=f32
+            ) * (1.0 / (math.sqrt(HEAD) * math.sqrt(rows * seqs)))
+            lp[origin] = logits.astype(bf16)
+            owner = origin // count_t
+            slot = rl.at[a, origin % count_t]
+
+            @pl.when(owner == a)
+            def _():
+                pltpu.make_async_copy(lp.at[origin], slot, in_seq.at[0]).start()
+
+            @pl.when(owner != a)
+            def _():
+                pltpu.make_async_remote_copy(
+                    lp.at[origin], slot, out_seq.at[0], in_seq.at[0],
+                    device_id={"seq": a_peer(owner)}, device_id_type=MESH,
+                ).start()
+
         send_values(FAR_FIRST[:3])
         arrived(rl, in_seq.at[0])
         total = jnp.sum(rl[...].astype(f32), axis=0)
@@ -218,16 +234,27 @@
         total = jnp.exp(total - jnp.max(total, axis=-1, keepdims=True))
         total = total / jnp.sum(total, axis=-1, keepdims=True)
         t4[...] = total.astype(bf16)
-        exchange(lambda peer: t4, rt, 2, a, n_a, a_peer)
+        for k in range(count_t):
+            pltpu.make_async_copy(t4.at[k], rt.at[a * count_t + k], in_t.at[a * count_t + k]).start()
+
+            def step(n, carry, k=k):
+                peer = lax.rem(a + n + core * (n_a - 2 * n), n_a)
+                pltpu.make_async_remote_copy(
+                    t4.at[k], rt.at[a * count_t + k], out_t, in_t.at[a * count_t + k],
+                    device_id={"seq": a_peer(peer)}, device_id_type=MESH,
+                ).start()
+                return carry
+
+            lax.fori_loop(1, n_a, step, 0)
         send_values(FAR_FIRST[6:])
         arrived(rv, in_v)
         values = jnp.concatenate([rv[:, r].reshape(everywhere, LANES) for r in range(quads)], axis=1)
-        arrived(rt, in_seq.at[2])
-        context = jnp.dot(rt[...].reshape(here, everywhere), values, preferred_element_type=f32)
-        for r in range(quads):
-            oc[:, r] = context[:, r * LANES : (r + 1) * LANES].reshape(Z, cols, LANES).astype(bf16)
         for offset in FAR_FIRST:
             peer = away(offset)
+            arrived(rt.at[peer], in_t.at[peer])
+            context = jnp.dot(rt[peer], values, preferred_element_type=f32).astype(bf16)
+            for r in range(quads):
+                oc[peer, r] = context[:, r * LANES : (r + 1) * LANES]
             if offset == 0:
                 pltpu.make_async_copy(oc.at[z], rc.at[head_here], in_c).start()
             else:
@@ -261,29 +288,53 @@
     arrived(rcs, in_seq.at[4])
 
     total_rows = seqs * rows
-    low = low_lanes((total_rows, LANES))
-    zero = jnp.zeros((total_rows, LANES), bf16)
+    parts = 2
+    some = total_rows // parts
+    low = low_lanes((some, LANES))
+    zero = jnp.zeros((some, LANES), bf16)
+    columns = []
     for c in range(per_device):
         update = jnp.dot(rcs[:, c].reshape(total_rows, INNER), wo_ref[...], preferred_element_type=f32)
         updated = (rx[:, c].reshape(total_rows, features).astype(f32) + update).astype(bf16)
         normed = layer_norm(updated.astype(f32), g2_ref[...].reshape(1, features)).astype(bf16)
-        packed = jnp.dot(normed, w2_ref[...], preferred_element_type=f32).astype(bf16)
-        for pair in range(HEADS // 2):
-            span = slice(pair * LANES, (pair + 1) * LANES)
-            query, key, value = (
-                packed[:, part * INNER + pair * LANES : part * INNER + (pair + 1) * LANES]
-                for part in range(3)
-            )
-            mixed = []
-            for mask in (low, jnp.logical_not(low)):
-                scores = lax.dot_general(
-                    jnp.where(mask, query, zero), key, (((1,), (1,)), ((), ())), preferred_element_type=f32
-                ) * (1.0 / math.sqrt(HEAD))
-                scores = jnp.exp(scores - jnp.max(scores, axis=-1, keepdims=True))
-                weights = (scores / jnp.sum(scores, axis=-1, keepdims=True)).astype(bf16)
-                mixed.append(jnp.dot(weights, value, preferred_element_type=f32))
-            ac[:, c, :, span] = jnp.where(low, mixed[0], mixed[1]).astype(bf16).reshape(seqs, rows, LANES)
-    exchange(lambda peer: ac.at[peer], ra, 5, s, seqs, s_peer)
+        columns.append(jnp.dot(normed, w2_ref[...], preferred_element_type=f32).astype(bf16))
+    for part in range(parts):
+        peers = seqs // parts
+        for c, packed in enumerate(columns):
+            for pair in range(HEADS // 2):
+                span = slice(pair * LANES, (pair + 1) * LANES)
+                query = packed[part * some : (part + 1) * some, span]
+                key = packed[:, INNER + pair * LANES : INNER + (pair + 1) * LANES]
+                value = packed[:, 2 * INNER + pair * LANES : 2 * INNER + (pair + 1) * LANES]
+                mixed = []
+                for mask in (low, jnp.logical_not(low)):
+                    scores = lax.dot_general(
+                        jnp.where(mask, query, zero), key, (((1,), (1,)), ((), ())), preferred_element_type=f32
+                    ) * (1.0 / math.sqrt(HEAD))
+                    scores = jnp.exp(scores - jnp.max(scores, axis=-1, keepdims=True))
+                    weights = (scores / jnp.sum(scores, axis=-1, keepdims=True)).astype(bf16)
+                    mixed.append(jnp.dot(weights, value, preferred_element_type=f32))
+                ac[part * peers : (part + 1) * peers, c, :, span] = (
+                    jnp.where(low, mixed[0], mixed[1]).astype(bf16).reshape(peers, rows, LANES)
+                )
+
+        def step(k, carry, part=part, peers=peers):
+            peer = part * peers + lax.rem(s + k, peers)
+
+            @pl.when(peer == s)
+            def _():
+                pltpu.make_async_copy(ac.at[s], ra.at[s], in_seq.at[5]).start()
+
+            @pl.when(peer != s)
+            def _():
+                pltpu.make_async_remote_copy(
+                    ac.at[peer], ra.at[s], out_seq.at[5], in_seq.at[5],
+                    device_id={"seq": peer}, device_id_type=MESH,
+                ).start()
+
+            return carry
+
+        lax.fori_loop(0, peers, step, 0)
     sent_head(1, out_k, True)
     sent_head(0, out_q, False)
     sent_head(2, out_v.at[0], False)
@@ -292,9 +343,9 @@
 
     @pl.when(worker)
     def _():
-        sent(rl, 0, n_a)
+        arrived(lp.at[pl.ds(0, Z - count_t)], out_seq.at[0])
         sent(r2, 1, n_b)
-        sent(rt, 2, n_a)
+        arrived(rt.at[pl.ds(0, Z - count_t)], out_t)
         arrived(oc.at[pl.ds(0, Z - 1)], out_c)
 
     sent(rx, 3, seqs)
@@ -338,12 +389,12 @@
             pltpu.VMEM((Z,) + head, bf16),
             pltpu.VMEM((res,) + head, bf16),
             pltpu.VMEM((res,) + head, bf16),
-            pltpu.VMEM((n_a, here // n_a, everywhere), bf16),
-            pltpu.VMEM((n_a, here // n_a, everywhere), bf16),
-            pltpu.VMEM((here // n_a, everywhere), bf16),
-            pltpu.VMEM((n_b, here // n_a, everywhere), bf16),
-            pltpu.VMEM((here // n_a, everywhere), bf16),
-            pltpu.VMEM((n_a, here // n_a, everywhere), bf16),
+            pltpu.VMEM((Z, cols, everywhere), bf16),
+            pltpu.VMEM((n_a, Z // n_a, cols, everywhere), bf16),
+            pltpu.VMEM((Z // n_a, cols, everywhere), bf16),
+            pltpu.VMEM((n_b, Z // n_a, cols, everywhere), bf16),
+            pltpu.VMEM((Z // n_a, cols, everywhere), bf16),
+            pltpu.VMEM((Z, cols, everywhere), bf16),
             pltpu.VMEM((Z,) + head, bf16),
             pltpu.VMEM((HEADS,) + head, bf16),
             pltpu.VMEM((seqs, per_device, rows, features), bf16),
@@ -358,11 +409,13 @@
             dma((2, HEADS, 1)),
             dma,
             dma,
-            dma,
-            dma,
-            dma,
-            dma,
-            dma,
+            dma((Z,)),
+            dma,
+            dma,
+            dma,
+            dma,
+            dma,
+            dma((Z,)),
             dma((6,)),
             dma((6,)),
         ],

time: 78.8 us -> 76.6 us (0.972)
  Pallas kernels: 76.6 us -> 74.5 us
    pallas_call x1, Pallas kernels: 76.6 us -> 74.5 us  [body(): pl.pallas_call(functools.partial(kernel, seqs), out_shape=(jax.ShapeDtype...]
where the time goes in v4:
time: 76.6 us; the launch traced here: 76.5 us
  Pallas kernels  74.5 us (97%)
  local copies, waits for them, and re-layouts  1.42 us (2%)
    pallas_call x1, Pallas kernels, body(): pl.pallas_call(functools.partial(kernel, seqs), out_shape=(jax.ShapeDtype...  74.5 us

profile of v4, /device:TPU:1, one launch (start us, length us, event | category | flops | bytes accessed | tf_op | source)
XLA Modules:
  0.0 76.5 jit_solution(14232216151263692492)
XLA Ops:
  0.6 74.5 %msa_layer.1 = (bf16[8,32,768]{2,1,0:T(8,128)(2,1)S(1)}, bf16[8,32,384]{2,1,0:T(8,128)(2,1)S(1)}) custom-call(bf16[8,32,768]{2,1,0:T(8,128)(2,1)} %x_hbm.1, bf16[768]{0:T(1024)(128)(2,1)} %g1_hbm.1, bf16[768,1152]{1,0:T(8,128)(2,1)} %w1_hbm.1, bf16[768]{0:T(1024)(128)(2,1)} %g2_hbm.1, bf16[384,768]{1,0:T(8,128)(2,1)} %wo_hbm.1, bf16[768,1152]{1,0:T(8,128)(2,1)} %w2_hbm.1), custom_call_target="tpu_custom_call" | custom-call | tf_op jit(solution)/shard_map/msa_layer/pallas_call | solution.py:373
  75.1 0.7 copy.10
  75.8 0.7 copy.11

commit v5 on v4

--- a/solution.py
+++ b/solution.py
@@ -23,6 +23,14 @@
     centred = values - average
     spread = jnp.mean(centred * centred, axis=-1, keepdims=True)
     return centred * lax.rsqrt(spread + 1e-05) * gain.astype(jnp.float32)
+
+
+def flipped(index, k, count):
+    both, bit = 0, 1
+    while bit < count:
+        both += ((index // bit) % 2) * ((k // bit) % 2) * bit
+        bit *= 2
+    return index + k - 2 * both
 
 
 def low_lanes(shape):
@@ -162,7 +170,7 @@
         pltpu.make_async_copy(block(me), dst.at[me], in_seq.at[stage]).start()
 
         def step(k, carry):
-            peer = lax.rem(me + k + core * (count - 2 * k), count)
+            peer = flipped(me, count - k, count)
             pltpu.make_async_remote_copy(
                 block(peer), dst.at[me], out_seq.at[stage], in_seq.at[stage],
                 device_id={"seq": peer_of(peer)}, device_id_type=MESH,
@@ -238,7 +246,7 @@
             pltpu.make_async_copy(t4.at[k], rt.at[a * count_t + k], in_t.at[a * count_t + k]).start()
 
             def step(n, carry, k=k):
-                peer = lax.rem(a + n + core * (n_a - 2 * n), n_a)
+                peer = flipped(a, n_a - n, n_a)
                 pltpu.make_async_remote_copy(
                     t4.at[k], rt.at[a * count_t + k], out_t, in_t.at[a * count_t + k],
                     device_id={"seq": a_peer(peer)}, device_id_type=MESH,
@@ -319,7 +327,7 @@
                 )
 
         def step(k, carry, part=part, peers=peers):
-            peer = part * peers + lax.rem(s + k, peers)
+            peer = part * peers + flipped(s % peers, peers - 1 - k, peers)
 
             @pl.when(peer == s)
             def _():

time: 76.6 us -> 76 us (level)
  Pallas kernels: 74.5 us -> 73.5 us
    pallas_call x1, Pallas kernels: 74.5 us -> 73.5 us  [body(): pl.pallas_call(functools.partial(kernel, seqs), out_shape=(jax.ShapeDtype...]
where the time goes in v5:
time: 76 us; the launch traced here: 75.6 us
  Pallas kernels  73.5 us (97%)
  local copies, waits for them, and re-layouts  1.42 us (2%)
    pallas_call x1, Pallas kernels, body(): pl.pallas_call(functools.partial(kernel, seqs), out_shape=(jax.ShapeDtype...  73.5 us

profile of v5, /device:TPU:1, one launch (start us, length us, event | category | flops | bytes accessed | tf_op | source)
XLA Modules:
  0.0 75.6 jit_solution(1512745160151900456)
XLA Ops:
  0.6 73.5 %msa_layer.1 = (bf16[8,32,768]{2,1,0:T(8,128)(2,1)S(1)}, bf16[8,32,384]{2,1,0:T(8,128)(2,1)S(1)}) custom-call(bf16[8,32,768]{2,1,0:T(8,128)(2,1)} %x_hbm.1, bf16[768]{0:T(1024)(128)(2,1)} %g1_hbm.1, bf16[768,1152]{1,0:T(8,128)(2,1)} %w1_hbm.1, bf16[768]{0:T(1024)(128)(2,1)} %g2_hbm.1, bf16[384,768]{1,0:T(8,128)(2,1)} %wo_hbm.1, bf16[768,1152]{1,0:T(8,128)(2,1)} %w2_hbm.1), custom_call_target="tpu_custom_call" | custom-call | tf_op jit(solution)/shard_map/msa_layer/pallas_call | solution.py:381
  74.2 0.7 copy.10
  74.9 0.7 copy.11

commit v6 on v5

--- a/solution.py
+++ b/solution.py
@@ -257,19 +257,22 @@
         send_values(FAR_FIRST[6:])
         arrived(rv, in_v)
         values = jnp.concatenate([rv[:, r].reshape(everywhere, LANES) for r in range(quads)], axis=1)
-        for offset in FAR_FIRST:
-            peer = away(offset)
-            arrived(rt.at[peer], in_t.at[peer])
-            context = jnp.dot(rt[peer], values, preferred_element_type=f32).astype(bf16)
-            for r in range(quads):
-                oc[peer, r] = context[:, r * LANES : (r + 1) * LANES]
-            if offset == 0:
-                pltpu.make_async_copy(oc.at[z], rc.at[head_here], in_c).start()
-            else:
-                pltpu.make_async_remote_copy(
-                    oc.at[peer], rc.at[head_here], out_c, in_c,
-                    device_id={"res": yh * Z + peer}, device_id_type=MESH,
-                ).start()
+        for group in (FAR_FIRST[:4], FAR_FIRST[4:]):
+            homes = [away(offset) for offset in group]
+            for home in homes:
+                arrived(rt.at[home], in_t.at[home])
+            tied = jnp.concatenate([rt[home] for home in homes], axis=0)
+            context = jnp.dot(tied, values, preferred_element_type=f32).astype(bf16)
+            for n, (offset, home) in enumerate(zip(group, homes)):
+                for r in range(quads):
+                    oc[home, r] = context[n * cols : (n + 1) * cols, r * LANES : (r + 1) * LANES]
+                if offset == 0:
+                    pltpu.make_async_copy(oc.at[z], rc.at[head_here], in_c).start()
+                else:
+                    pltpu.make_async_remote_copy(
+                        oc.at[home], rc.at[head_here], out_c, in_c,
+                        device_id={"res": yh * Z + home}, device_id_type=MESH,
+                    ).start()
 
     exchange(lambda peer: xs.at[peer], rx, 3, s, seqs, s_peer)
     arrived(rc, in_c)

time: 76 us -> 75.4 us (level)
  no operation moved by 1% of the time
where the time goes in v6:
time: 75.4 us; the launch traced here: 75.3 us
  Pallas kernels  73.2 us (97%)
  local copies, waits for them, and re-layouts  1.42 us (2%)
    pallas_call x1, Pallas kernels, body(): pl.pallas_call(functools.partial(kernel, seqs), out_shape=(jax.ShapeDtype...  73.2 us

profile of v6, /device:TPU:1, one launch (start us, length us, event | category | flops | bytes accessed | tf_op | source)
XLA Modules:
  0.0 75.3 jit_solution(13267141251315280812)
XLA Ops:
  0.6 73.2 %msa_layer.1 = (bf16[8,32,768]{2,1,0:T(8,128)(2,1)S(1)}, bf16[8,32,384]{2,1,0:T(8,128)(2,1)S(1)}) custom-call(bf16[8,32,768]{2,1,0:T(8,128)(2,1)} %x_hbm.1, bf16[768]{0:T(1024)(128)(2,1)} %g1_hbm.1, bf16[768,1152]{1,0:T(8,128)(2,1)} %w1_hbm.1, bf16[768]{0:T(1024)(128)(2,1)} %g2_hbm.1, bf16[384,768]{1,0:T(8,128)(2,1)} %wo_hbm.1, bf16[768,1152]{1,0:T(8,128)(2,1)} %w2_hbm.1), custom_call_target="tpu_custom_call" | custom-call | tf_op jit(solution)/shard_map/msa_layer/pallas_call | solution.py:384
  73.8 0.7 copy.10
  74.6 0.7 copy.11
